TPU v7x, 32 devices: a whole 2x2x4 slice. The times are simulated.
32 devices in a mesh: pool: 8 (over y, x, core), head: 4 (over z).
Axes of the slice: x: 2, y: 2, z: 4, core: 2. Of those that a mesh axis runs over, the one named last changes fastest.
Arguments:
- x_rows: bfloat16 [256, 4096], P('pool'), may hold values from -3 to 3
- query: bfloat16 [256, 4096], P('pool', 'head'), may hold values from -170 to 170
- key_cache: bfloat16 [256, 4, 512, 128], P('pool', 'head'), may hold values from -6 to 6
- value_cache: bfloat16 [256, 4, 512, 128], P('pool', 'head'), may hold values from -6 to 6
- new_key: bfloat16 [256, 512], P('pool', 'head'), may hold values from -6 to 6
- new_value: bfloat16 [256, 512], P('pool', 'head'), may hold values from -6 to 6
- lengths: int32 [256], P('pool'), may hold values from 2 to 512, as said below
- out_proj: bfloat16 [4096, 4096], P('head'), may hold values from -0.5 to 0.5
- norm_gain: float32 [4096], replicated, may hold values from 0.5 to 1.5
- expert_ids: int32 [256, 8], P('pool'), may hold values from 0 to 15, all different within a row; in each aligned block of 32 rows (0 to 31, 32 to 63, ...) at most 32 rows name the same one
- gate_weights: float32 [256, 8], P('pool'), may hold values from 0.05 to 1
- w_gate: bfloat16 [16, 4096, 1024], P('pool', None, 'head'), may hold values from -0.09375 to 0.09375
- w_up: bfloat16 [16, 4096, 1024], P('pool', None, 'head'), may hold values from -0.09375 to 0.09375
- w_down: bfloat16 [16, 1024, 4096], P('pool', 'head'), may hold values from -0.1875 to 0.1875
Outputs:
- layer_out: bfloat16 [256, 4096], P('pool', 'head')
Inputs may be any that keep to these rules, and one draw needn't show every extreme that they name: `expert_ids`: within the 32 requests of one index of pool, no expert is named by more than 32 pairs, a bound that some block reaches. `lengths`: request 0 uses all 512 slots.
All inputs are finite; a program needn't handle non-finite values.
Results may differ from a plain program's by a relative error of at most 0.017.
Values may be sent and summed in bfloat16 or wider, within the bound.
A program may use at most 128 MiB of HBM per device.

v0:
```python
import jax
import jax.numpy as jnp
from jax import lax
from jax.sharding import PartitionSpec as P


def attend(query, key_cache, value_cache, new_key, new_value, lengths):
    token_count = query.shape[0]
    head_size = new_key.shape[1]
    queries = query.reshape(token_count, -1, head_size)
    cached_keys = key_cache[:, 0]
    cached_values = value_cache[:, 0]
    score_scale = head_size ** (-0.5)
    scores = (
        jnp.einsum("rqd,rcd->rqc", queries, cached_keys, preferred_element_type=jnp.float32)
        * score_scale
    )
    fresh_score = (
        jnp.einsum("rqd,rd->rq", queries, new_key, preferred_element_type=jnp.float32) * score_scale
    )
    live_mask = (jnp.arange(cached_keys.shape[1])[None, :] < lengths[:, None])[:, None, :]
    scores = jnp.where(live_mask, scores, -1e30)
    highest = jnp.maximum(jnp.max(scores, -1), fresh_score)
    weights = jnp.where(live_mask, jnp.exp(scores - highest[..., None]), 0.0)
    own_term = jnp.exp(fresh_score - highest)
    totals = jnp.sum(weights, -1) + own_term
    probs = (weights / totals[..., None]).astype(jnp.bfloat16)
    own_prob = (own_term / totals).astype(jnp.bfloat16)
    mixed = jnp.einsum("rqc,rcd->rqd", probs, cached_values, preferred_element_type=jnp.float32)
    mixed = (
        mixed + own_prob.astype(jnp.float32)[..., None] * new_value.astype(jnp.float32)[:, None, :]
    )
    return mixed.astype(jnp.bfloat16).reshape(token_count, -1)


def route_tables(expert_ids, gate_weights, experts, capacity):
    token_count, choose = expert_ids.shape
    flat_ids = expert_ids.reshape(-1)
    one_hot = (flat_ids[:, None] == jnp.arange(experts)[None, :]).astype(jnp.int32)
    earlier = jnp.cumsum(one_hot, 0) - one_hot
    ranking = jnp.sum(earlier * one_hot, 1)
    slot_index = flat_ids * capacity + ranking
    matching = (jnp.arange(experts * capacity)[:, None] == slot_index[None, :]).reshape(
        experts * capacity, token_count, choose
    )
    send_table = jnp.sum(matching.astype(jnp.float32), 2).astype(jnp.bfloat16)
    take_table = jnp.sum(jnp.where(matching, gate_weights[None, :, :], 0.0), 2).T
    return (send_table, take_table)


def experts_apply(arrived, w_gate, w_up, w_down):
    gate_part = jnp.einsum("secd,edf->secf", arrived, w_gate, preferred_element_type=jnp.float32)
    up_part = jnp.einsum("secd,edf->secf", arrived, w_up, preferred_element_type=jnp.float32)
    act = (jax.nn.silu(gate_part) * up_part).astype(jnp.bfloat16)
    return jnp.einsum("secf,efd->secd", act, w_down, preferred_element_type=jnp.float32)


def body(
    x_rows,
    query,
    key_cache,
    value_cache,
    new_key,
    new_value,
    lengths,
    out_proj,
    norm_gain,
    expert_ids,
    gate_weights,
    w_gate,
    w_up,
    w_down,
):
    pools = lax.axis_size("pool")
    groups = lax.axis_size("head")
    width = x_rows.shape[1]
    share = width // groups
    local_experts = w_gate.shape[0]
    all_experts = pools * local_experts
    capacity = max(2, 2 * expert_ids.shape[0] * expert_ids.shape[1] // all_experts)
    attn = attend(query, key_cache, value_cache, new_key, new_value, lengths)
    partial_value = jnp.dot(attn, out_proj, preferred_element_type=jnp.float32)
    send_table, take_table = route_tables(expert_ids, gate_weights, all_experts, capacity)
    offset = lax.axis_index("head") * share
    hidden = x_rows.astype(jnp.float32) + lax.psum(
        partial_value.astype(jnp.bfloat16), "head"
    ).astype(jnp.float32)
    mean_square = jnp.mean(hidden * hidden, -1, keepdims=True)
    normed = (hidden * lax.rsqrt(mean_square + 1e-06) * norm_gain[None, :]).astype(jnp.bfloat16)
    outgoing = (
        jnp.dot(send_table, normed, preferred_element_type=jnp.float32)
        .astype(jnp.bfloat16)
        .reshape(pools, -1, width)
    )
    arrived = lax.all_to_all(outgoing, "pool", split_axis=0, concat_axis=0, tiled=True)
    produced = experts_apply(
        arrived.reshape(pools, local_experts, capacity, width), w_gate, w_up, w_down
    )
    produced = lax.psum(produced.astype(jnp.bfloat16), "head")
    returned = lax.all_to_all(
        produced.reshape(pools, -1, width), "pool", split_axis=0, concat_axis=0, tiled=True
    )
    moe_sum = jnp.dot(
        take_table, returned.reshape(-1, width).astype(jnp.float32), precision=lax.Precision.HIGHEST
    )
    finished = hidden + moe_sum
    return lax.dynamic_slice_in_dim(finished, offset, share, 1).astype(jnp.bfloat16)


def solution(mesh):
    placed = (
        P("pool", None),
        P("pool", "head"),
        P("pool", "head", None, None),
        P("pool", "head", None, None),
        P("pool", "head"),
        P("pool", "head"),
        P("pool"),
        P("head", None),
        P(),
        P("pool", None),
        P("pool", None),
        P("pool", None, "head"),
        P("pool", None, "head"),
        P("pool", "head", None),
    )
    return jax.shard_map(
        body, mesh=mesh, in_specs=placed, out_specs=P("pool", "head"), check_vma=False
    )
```

profile of v0, /device:TPU:0, one launch (start us, length us, event | category | flops | bytes accessed | tf_op | source)
XLA Modules:
  0.0 347.4 jit_solution(4041421373729813538)
XLA Ops:
  6.5 0.9 copy.38
  7.4 0.7 iota_compare_fusion.1
  8.2 0.1 fusion.68
  8.3 3.6 %fusion.75 = (f32[32,8]{1,0:T(8,128)S(1)}, f32[32,8,512]{2,1,0:T(8,128)S(1)}) fusion(bf16[32,8,128]{2,1,0:T(8,128)(2,1)S(1)} %bitcast.98, bf16[32,1,512,128]{3,2,1,0:T(8,128)(2,1)} %param.16, pred[32,512]{1,0:T(8,128)(4,1)S(1)} %iota_compare_fusion.1), kind=kOutput, calls=%fused_computation.70 | convolution fusion | flops 33947392 | bytes 4801536 | tf_op jit(solution)/shard_map/rqd,rcd->rqc/dot_general | solution.py:15
  11.9 0.3 fusion.53
  12.3 2.9 fusion.45
  15.2 2.2 convolution_convert_fusion.2
  17.5 0.0 all-reduce.3.cloned.1.call-update
  17.5 0.0 all-reduce.5.cloned.1.call-start
  17.6 0.1 copy.24
  17.7 0.1 eq.40
  17.7 0.1 eq.44
  17.8 0.6 reduce-window.6
  18.4 0.2 slice_reduce_fusion
  18.7 0.1 fusion.67
  18.8 0.1 reduce_sum.49
  18.9 0.1 copy.28
  18.9 0.4 convert_reduce_fusion
  19.3 36.3 %all-reduce.3.cloned.1.call-done = bf16[32,4096]{1,0:T(8,128)(2,1)} async-done(((bf16[32,4096]{1,0:T(8,128)(2,1)}), bf16[32,4096]{1,0:T(8,128)(2,1)}) %all-reduce.3.cloned.1.call-update) | async-done | bytes 262160 | tf_op jit(solution)/shard_map/psum | solution.py:85
  55.7 1.2 convert_add_fusion
  56.9 2.3 convolution_convert_fusion.1
  59.1 52.8 %all_to_all.10 = bf16[8,64,4096]{2,1,0:T(8,128)(2,1)S(1)} all-to-all(bf16[8,64,4096]{2,1,0:T(8,128)(2,1)S(1)} %bitcast.93), channel_id=1, replica_groups=mesh['pool'=8,'head'=4] {'pool'}, dimensions={0} | all-to-all | bytes 8388608 | tf_op jit(solution)/shard_map/all_to_all | solution.py:95
  111.9 2.0 copy-done.2
  113.9 1.2 fusion.18
  115.1 9.0 %fusion = bf16[8,2,32,4096]{3,2,0,1:T(8,128)(2,1)} fusion(bf16[2,256,4096]{2,1,0:T(8,128)(2,1)} %param.27, bf16[2,4096,256]{2,1,0:T(8,128)(2,1)} %param.26, bf16[8,2,32,4096]{3,2,1,0:T(8,128)(2,1)} %bitcast.95, f32[8,2,32,256]{3,2,0,1:T(8,128)S(1)} %fusion.18), kind=kOutput, calls=%fused_computation.2 | convolution fusion | flops 2150367232 | bytes 17301504 | tf_op jit(solution)/shard_map/secf,efd->secd/dot_general | solution.py:55
  124.2 4.7 %copy.31 = bf16[8,2,32,4096]{3,2,1,0:T(8,128)(2,1)} copy(bf16[8,2,32,4096]{3,2,0,1:T(8,128)(2,1)} %fusion) | data formatting | bytes 8388608 | tf_op jit(solution)/shard_map/convert_element_type | solution.py:99
  128.8 0.0 all-reduce.5.cloned.1.call-update
  128.9 153.1 %all-reduce.5.cloned.1.call-done = bf16[8,64,4096]{2,1,0:T(8,128)(2,1)} async-done(((bf16[8,64,4096]{2,1,0:T(8,128)(2,1)}), bf16[8,64,4096]{2,1,0:T(8,128)(2,1)}) %all-reduce.5.cloned.1.call-update) | async-done | bytes 4194320 | tf_op jit(solution)/shard_map/psum | solution.py:99
  281.9 4.5 %all-to-all-start.1 = ((bf16[8,64,4096]{2,1,0:T(8,128)(2,1)}), bf16[8,64,4096]{2,1,0:T(8,128)(2,1)}, u32[]{:S(2)}, u32[]{:S(2)}) async-start(bf16[8,64,4096]{2,1,0:T(8,128)(2,1)} %all-reduce.5.cloned.1.call-done), calls=%async_computation.1 | async-start | bytes 8388608 | tf_op jit(solution)/shard_map/all_to_all | solution.py:100
  286.5 49.1 %all-to-all-done.1 = bf16[8,64,4096]{2,1,0:T(8,128)(2,1)} async-done(((bf16[8,64,4096]{2,1,0:T(8,128)(2,1)}), bf16[8,64,4096]{2,1,0:T(8,128)(2,1)}, u32[]{:S(2)}, u32[]{:S(2)}) %all-to-all-start.1) | async-done | bytes 4194336 | tf_op jit(solution)/shard_map/all_to_all | solution.py:100
  335.6 4.3 %fusion.76 = f32[32,4096]{1,0:T(8,128)S(1)} fusion(f32[512,32]{0,1:T(8,128)S(1)} %get-tuple-element.6, bf16[512,4096]{1,0:T(8,128)(2,1)} %bitcast.18), kind=kOutput, calls=%fused_computation.71 | convolution fusion | flops 805306368 | bytes 4784128 | tf_op jit(solution)/shard_map/dot_general | solution.py:103
  339.9 0.7 fusion.61
  (26 shorter events, 0.1 us)
Async XLA Ops:
  6.5 1.6 copy-start
  6.5 5.7 %copy-start.5 = (bf16[32,128]{1,0:T(8,128)(2,1)S(1)}, bf16[32,128]{1,0:T(8,128)(2,1)}, u32[]{:S(2)}) copy-start(bf16[32,128]{1,0:T(8,128)(2,1)} %param.19) | copy-start | bytes 24580
  6.5 49.1 %all-reduce.3.cloned.1.call-start = ((), (), s32[]{:S(2)}) async-start(), calls=%async_computation.2 | async-start | bytes 524288 | tf_op jit(solution)/shard_map/psum | solution.py:85
  8.3 6.9 %copy-start.1 = (bf16[1024,4096]{1,0:T(8,128)(2,1)S(1)}, bf16[1024,4096]{1,0:T(8,128)(2,1)}, u32[]{:S(2)}) copy-start(bf16[1024,4096]{1,0:T(8,128)(2,1)} %param.21) | copy-start | bytes 25165828
  15.2 2.4 copy-start.6
  15.2 3.6 %copy-start.7 = (f32[32,8]{0,1:T(8,128)S(1)}, f32[32,8]{0,1:T(8,128)}, u32[]{:S(2)}) copy-start(f32[32,8]{0,1:T(8,128)} %param.24) | copy-start | bytes 3076
  15.2 40.5 %copy-start.3 = (bf16[32,4096]{1,0:T(8,128)(2,1)S(1)}, bf16[32,4096]{1,0:T(8,128)(2,1)}, u32[]{:S(2)}) copy-start(bf16[32,4096]{1,0:T(8,128)(2,1)} %param.14) | copy-start | bytes 786436
  15.2 41.6 %copy-start.4 = (f32[4096]{0:T(1024)S(1)}, f32[4096]{0:T(1024)}, u32[]{:S(2)}) copy-start(f32[4096]{0:T(1024)} %param.22) | copy-start | bytes 49156
  17.5 264.4 %all-reduce.5.cloned.1.call-start = ((), (), s32[]{:S(2)}) async-start(), calls=%async_computation.3 | async-start | bytes 8388608 | tf_op jit(solution)/shard_map/psum | solution.py:99
  59.1 54.8 %copy-start.8 = (bf16[2,4096,256]{2,1,0:T(8,128)(2,1)S(1)}, bf16[2,4096,256]{2,1,0:T(8,128)(2,1)}, u32[]{:S(2)}) copy-start(bf16[2,4096,256]{2,1,0:T(8,128)(2,1)} %param.25) | copy-start | bytes 12582916
  111.9 2.0 copy-start.2
  281.9 53.7 %all-to-all-start.1 = ((bf16[8,64,4096]{2,1,0:T(8,128)(2,1)}), bf16[8,64,4096]{2,1,0:T(8,128)(2,1)}, u32[]{:S(2)}, u32[]{:S(2)}) async-start(bf16[8,64,4096]{2,1,0:T(8,128)(2,1)} %all-reduce.5.cloned.1.call-done), calls=%async_computation.1 | async-start | bytes 8388608 | tf_op jit(solution)/shard_map/all_to_all | solution.py:100
Sparse Core Ops, SparseCore 0:
  17.6 37.9 all-reduce.2
  129.0 152.8 all-reduce.4
where the time goes:
time: 348 us; the launch traced here: 347 us
  waiting for transfers between devices  239 us (69%)
  blocking collectives  52.8 us (15%)
  matrix products  25.8 us (7%)
  between operations  13.6 us (4%)
  local copies, waits for them, and re-layouts  8.15 us (2%)
  starting transfers between devices  4.59 us (1%)
  other arithmetic  3.98 us (1%)
    psum x1, waiting for transfers between devices, body(): produced = lax.psum(produced.astype(jnp.bfloat16), 'head')  153 us
    all_to_all x1, blocking collectives, body(): lax.all_to_all(outgoing, 'pool', split_axis=0, concat_axis=0, tiled=True)  52.8 us
    all_to_all x1, waiting for transfers between devices, body(): lax.all_to_all(produced.reshape(pools, -1, width), 'pool', split_axis=0,...  49.1 us
    psum x1, waiting for transfers between devices, body(): lax.psum(partial_value.astype(jnp.bfloat16), 'head').astype(jnp.float32)  36.3 us
    dot_general x1, matrix products, experts_apply(): jnp.einsum('secf,efd->secd', act, w_down, preferred_element_type=jnp.floa...  9.05 us
  transfers between devices with their start and end apart: 3, of which 3 were waited for; matrix products, arithmetic and copies ran while one was open for 0% of the time, Pallas kernels for 0%

commit v1 on v0

v1 whole, which is shorter than its diff:
```python
import functools

import jax
import jax.numpy as jnp
from jax import lax
from jax.experimental import pallas as pl
from jax.experimental.pallas import tpu as pltpu
from jax.sharding import PartitionSpec as P

VMEM_BYTES = 60 * 1024 * 1024


def attend(query, key_cache, value_cache, new_key, new_value, lengths):
    token_count = query.shape[0]
    head_size = new_key.shape[1]
    queries = query.reshape(token_count, -1, head_size)
    cached_keys = key_cache[:, 0]
    cached_values = value_cache[:, 0]
    score_scale = head_size ** (-0.5)
    scores = (
        jnp.einsum("rqd,rcd->rqc", queries, cached_keys, preferred_element_type=jnp.float32)
        * score_scale
    )
    fresh_score = (
        jnp.einsum("rqd,rd->rq", queries, new_key, preferred_element_type=jnp.float32) * score_scale
    )
    live_mask = (jnp.arange(cached_keys.shape[1])[None, :] < lengths[:, None])[:, None, :]
    scores = jnp.where(live_mask, scores, -1e30)
    highest = jnp.maximum(jnp.max(scores, -1), fresh_score)
    weights = jnp.where(live_mask, jnp.exp(scores - highest[..., None]), 0.0)
    own_term = jnp.exp(fresh_score - highest)
    totals = jnp.sum(weights, -1) + own_term
    probs = (weights / totals[..., None]).astype(jnp.bfloat16)
    own_prob = (own_term / totals).astype(jnp.bfloat16)
    mixed = jnp.einsum("rqc,rcd->rqd", probs, cached_values, preferred_element_type=jnp.float32)
    mixed = (
        mixed + own_prob.astype(jnp.float32)[..., None] * new_value.astype(jnp.float32)[:, None, :]
    )
    return mixed.astype(jnp.bfloat16).reshape(token_count, -1)


MESH = pl.DeviceIdType.MESH
F32 = jnp.float32
BF16 = jnp.bfloat16


def flip(index, offset, count):
    result, bit = 0, 1
    while bit < count:
        result = result + bit * ((index // bit + offset // bit) % 2)
        bit *= 2
    return result


def layer_kernel(
    pools,
    groups,
    experts,
    attn_ref,
    x_ref,
    gates_ref,
    gain_ref,
    proj_hbm,
    gate_hbm,
    up_hbm,
    down_hbm,
    out_ref,
    proj,
    gate,
    up,
    down,
    part_send,
    part_recv,
    hidden,
    slabs,
    rows_all,
    act,
    produced,
    pair_recv,
    plane_send,
    plane_recv,
    last_send,
    last_recv,
    load_sem,
    part_sems,
    slab_sems,
    gather_sems,
    pair_sems,
    swap_sems,
    plane_sems,
    last_sems,
):
    chips = pools // 2
    rows, share = hidden.shape
    width = groups * share
    local = gate.shape[0]
    units = gate.shape[3]
    pool, head = lax.axis_index("pool"), lax.axis_index("head")
    chip, core = pool // 2, pool % 2
    partner = {"pool": chip * 2 + 1 - core}
    above = [{"head": (head + k) % groups} for k in range(groups)]
    across = [{"pool": flip(chip, q, chips) * 2 + core} for q in range(chips)]
    order = list(range(1, groups)) + [0]

    def send(source, target, sems, place, device):
        copy = pltpu.make_async_remote_copy(
            src_ref=source,
            dst_ref=target,
            send_sem=sems.at[(0,) + place],
            recv_sem=sems.at[(1,) + place],
            device_id=device,
            device_id_type=MESH,
        )
        copy.start()
        return copy

    loads = {}

    def load(name, index, source, target):
        copy = pltpu.make_async_copy(source, target, load_sem.at[len(loads)])
        copy.start()
        loads[name, index] = copy

    def columns(k):
        return pl.ds(pl.multiple_of((head + k) % groups * share, share), share)

    def depths(k):
        return pl.ds(pl.multiple_of((head - k + groups) % groups * share, share), share)

    for k in order:
        load("proj", k, proj_hbm.at[:, columns(k)], proj.at[k])
    for k in range(groups):
        for e in range(local):
            load("gate", (e, k), gate_hbm.at[e, depths(k)], gate.at[e, k])
            load("up", (e, k), up_hbm.at[e, depths(k)], up.at[e, k])
    for k in order:
        for e in range(local):
            load("down", (e, k), down_hbm.at[e, :, columns(k)], down.at[k, e])

    barrier = pltpu.get_barrier_semaphore()
    greeted = above[1:] + across[1:] + [partner]
    for device in greeted:
        pl.semaphore_signal(barrier, inc=1, device_id=device, device_id_type=MESH)
    pl.semaphore_wait(barrier, len(greeted))

    sent = []

    parts = {}
    for k in order:
        loads["proj", k].wait()
        term = jnp.dot(attn_ref[...], proj[k], preferred_element_type=F32)
        if k:
            part_send[k] = term.astype(BF16)
            parts[k] = send(part_send.at[k], part_recv.at[k], part_sems, (k,), above[k])
        else:
            own = pl.ds(pl.multiple_of(head * share, share), share)
            hidden[...] = term + x_ref[:, own].astype(F32)
    total = hidden[...]
    for k in order[:-1]:
        parts[k].wait_recv()
        total = total + part_recv[k].astype(F32)
    hidden[...] = total
    slabs[0] = total.astype(BF16)

    shared = {k: send(slabs.at[0], slabs.at[k], slab_sems, (k,), above[k]) for k in order[:-1]}
    for k in order[:-1]:
        shared[k].wait_recv()
    squares = jnp.zeros((rows, 1), F32)
    for k in range(groups):
        value = slabs[k].astype(F32)
        squares = squares + jnp.sum(value * value, -1, keepdims=True)
    scale = lax.rsqrt(squares / width + 1e-06)
    for k in range(groups):
        slab_gain = gain_ref[(head - k + groups) % groups]
        rows_all[0, :, k * share : (k + 1) * share] = (
            slabs[k].astype(F32) * scale * slab_gain
        ).astype(BF16)
    rows_all[0, :, width:] = gates_ref[...]

    gathers = {
        q: send(rows_all.at[0], rows_all.at[q], gather_sems, (q,), across[q])
        for q in range(1, chips)
    }
    pairs = [send(rows_all.at[0], rows_all.at[chips], pair_sems, (0,), partner)]
    for q in range(1, chips):
        gathers[q].wait_recv()
        pairs.append(
            send(rows_all.at[q], rows_all.at[chips + q], pair_sems, (q,), partner)
        )
    for copy in pairs:
        copy.wait_recv()

    block = min(8, pools)
    for name in ("gate", "up"):
        for k in range(groups):
            for e in range(local):
                loads[name, (e, k)].wait()

    def expert_rows(index, carry):
        place = pl.ds(index * block, block)
        gates = rows_all[place, :, width:].reshape(block * rows, -1).astype(F32)
        lane = lax.broadcasted_iota(jnp.int32, gates.shape, 1)
        for e in range(local):
            gate_part = jnp.zeros((block * rows, units), F32)
            up_part = jnp.zeros((block * rows, units), F32)
            for k in range(groups):
                piece = rows_all[place, :, k * share : (k + 1) * share].reshape(
                    block * rows, share
                )
                gate_part += jnp.dot(piece, gate[e, k], preferred_element_type=F32)
                up_part += jnp.dot(piece, up[e, k], preferred_element_type=F32)
            expert = pool * local + e
            chosen = (lane == expert) | (lane == experts + expert)
            weight = jnp.sum(jnp.where(chosen, gates, 0.0), -1, keepdims=True)
            value = gate_part / (1.0 + jnp.exp(-gate_part)) * up_part * weight
            act[place, :, e * units : (e + 1) * units] = value.astype(BF16).reshape(
                block, rows, units
            )
        return carry

    lax.fori_loop(0, pools // block, expert_rows, 0)

    swaps, planes, lasts = {}, {}, {}

    def project(k):
        for e in range(local):
            loads["down", (e, k)].wait()

        def down_rows(index, carry):
            place = pl.ds(index * block, block)
            value = jnp.dot(
                act[place].reshape(block * rows, local * units),
                down[k].reshape(local * units, share),
                preferred_element_type=F32,
            )
            produced[k, place] = value.astype(BF16).reshape(block, rows, share)
            return carry

        lax.fori_loop(0, pools // block, down_rows, 0)
        swaps[k] = send(
            produced.at[k, pl.ds(chips, chips)], pair_recv.at[k], swap_sems, (k,), partner
        )

    def cross(k):
        swaps[k].wait_recv()
        for q in range(1, chips):
            plane_send[k, q] = (
                produced[k, q].astype(F32) + pair_recv[k, q].astype(F32)
            ).astype(BF16)
            planes[k, q] = send(
                plane_send.at[k, q], plane_recv.at[k, q], plane_sems, (k, q), across[q]
            )

    def finish(k):
        value = produced[k, 0].astype(F32) + pair_recv[k, 0].astype(F32)
        for q in range(1, chips):
            planes[k, q].wait_recv()
            value = value + plane_recv[k, q].astype(F32)
        if k:
            last_send[k] = value.astype(BF16)
            lasts[k] = send(last_send.at[k], last_recv.at[k], last_sems, (k,), above[k])
        else:
            value = value + hidden[...]
            for j in order[:-1]:
                lasts[j].wait_recv()
                value = value + last_recv[j].astype(F32)
            out_ref[...] = value.astype(BF16)

    for step in range(groups + 2):
        if step < groups:
            project(order[step])
        if 1 <= step <= groups:
            cross(order[step - 1])
        if step >= 2:
            finish(order[step - 2])

    for group in (parts, shared, gathers, swaps, planes, lasts):
        for copy in group.values():
            copy.wait_send()
    for copy in pairs:
        copy.wait_send()


def gate_table(expert_ids, gate_weights, experts):
    matching = expert_ids[:, :, None] == jnp.arange(experts)[None, None, :]
    table = jnp.sum(jnp.where(matching, gate_weights[:, :, None], 0.0), 1)
    first = lax.reduce_precision(table, 8, 7)
    rest = table - first
    lanes = -(-2 * experts // 128) * 128
    both = jnp.concatenate([first, rest], 1).astype(BF16)
    return jnp.pad(both, ((0, 0), (0, lanes - 2 * experts)))


def body(
    x_rows,
    query,
    key_cache,
    value_cache,
    new_key,
    new_value,
    lengths,
    out_proj,
    norm_gain,
    expert_ids,
    gate_weights,
    w_gate,
    w_up,
    w_down,
):
    pools = lax.axis_size("pool")
    groups = lax.axis_size("head")
    rows, width = x_rows.shape
    share = width // groups
    local, _, units = w_gate.shape
    experts = pools * local
    chips = pools // 2
    attn = attend(query, key_cache, value_cache, new_key, new_value, lengths)
    gates = gate_table(expert_ids, gate_weights, experts)
    lanes = gates.shape[1]
    depth = out_proj.shape[0]
    in_vmem = pl.BlockSpec(memory_space=pltpu.VMEM)
    in_hbm = pl.BlockSpec(memory_space=pl.ANY)
    dma = pltpu.SemaphoreType.DMA
    return pl.pallas_call(
        functools.partial(layer_kernel, pools, groups, experts),
        out_shape=jax.ShapeDtypeStruct((rows, share), BF16),
        in_specs=[in_vmem] * 4 + [in_hbm] * 4,
        out_specs=in_vmem,
        scratch_shapes=[
            pltpu.VMEM((groups, depth, share), BF16),
            pltpu.VMEM((local, groups, share, units), BF16),
            pltpu.VMEM((local, groups, share, units), BF16),
            pltpu.VMEM((groups, local, units, share), BF16),
            pltpu.VMEM((groups, rows, share), BF16),
            pltpu.VMEM((groups, rows, share), BF16),
            pltpu.VMEM((rows, share), F32),
            pltpu.VMEM((groups, rows, share), BF16),
            pltpu.VMEM((pools, rows, width + lanes), BF16),
            pltpu.VMEM((pools, rows, local * units), BF16),
            pltpu.VMEM((groups, pools, rows, share), BF16),
            pltpu.VMEM((groups, chips, rows, share), BF16),
            pltpu.VMEM((groups, chips, rows, share), BF16),
            pltpu.VMEM((groups, chips, rows, share), BF16),
            pltpu.VMEM((groups, rows, share), BF16),
            pltpu.VMEM((groups, rows, share), BF16),
            dma((groups * (1 + 3 * local),)),
            dma((2, groups)),
            dma((2, groups)),
            dma((2, chips)),
            dma((2, chips)),
            dma((2, groups)),
            dma((2, groups, chips)),
            dma((2, groups)),
        ],
        compiler_params=pltpu.CompilerParams(
            collective_id=0, has_side_effects=True, vmem_limit_bytes=VMEM_BYTES
        ),
    )(
        attn,
        x_rows,
        gates,
        norm_gain.reshape(groups, 1, share),
        out_proj,
        w_gate,
        w_up,
        w_down,
    )


def solution(mesh):
    placed = (
        P("pool", None),
        P("pool", "head"),
        P("pool", "head", None, None),
        P("pool", "head", None, None),
        P("pool", "head"),
        P("pool", "head"),
        P("pool"),
        P("head", None),
        P(),
        P("pool", None),
        P("pool", None),
        P("pool", None, "head"),
        P("pool", None, "head"),
        P("pool", "head", None),
    )
    return jax.shard_map(
        body, mesh=mesh, in_specs=placed, out_specs=P("pool", "head"), check_vma=False
    )
```

time: 348 us -> 65.5 us (0.19)
  waiting for transfers between devices: 239 us -> 0 us
  Pallas kernels: 0 us -> 55.5 us
  blocking collectives: 52.8 us -> 0 us
  matrix products: 25.8 us -> 4.35 us
  between operations: 13.6 us -> 0.09 us
  local copies, waits for them, and re-layouts: 8.15 us -> 3.56 us
  starting transfers between devices: 4.59 us -> 0 us
    psum x2 -> x0, waiting for transfers between devices: 189 us -> none  [the longest x1 153 us: body(): produced = lax.psum(produced.astype(jnp.bfloat16), 'head')]
    pallas_call x0 -> x1, Pallas kernels: none -> 55.5 us  [body(): pl.pallas_call(functools.partial(layer_kernel, pools, groups, experts), o...]
    all_to_all x1 -> x0, blocking collectives: 52.8 us -> none  [body(): lax.all_to_all(outgoing, 'pool', split_axis=0, concat_axis=0, tiled=True)]
    all_to_all x1 -> x0, waiting for transfers between devices: 49.1 us -> none  [body(): lax.all_to_all(produced.reshape(pools, -1, width), 'pool', split_axis=0,...]
    dot_general x5 -> x0, matrix products: 19.1 us -> none  [the longest x1 9.05 us: experts_apply(): jnp.einsum('secf,efd->secd', act, w_down, preferred_element_type=jnp.floa...]
    convert_element_type x1 -> x0, local copies, waits for them, and re-layouts: 4.65 us -> none  [body(): produced = lax.psum(produced.astype(jnp.bfloat16), 'head')]
    all_to_all x1 -> x0, starting transfers between devices: 4.55 us -> none  [body(): lax.all_to_all(produced.reshape(pools, -1, width), 'pool', split_axis=0,...]
  transfers between devices with their start and end apart: 3 -> 0, of which waited for: 3 -> 0; matrix products, arithmetic and copies ran while one was open for 0% -> 0% of each run, Pallas kernels for 0% -> 0%
where the time goes in v1:
time: 65.5 us; the launch traced here: 65.3 us
  Pallas kernels  55.5 us (85%)
  matrix products  4.35 us (7%)
  local copies, waits for them, and re-layouts  3.56 us (5%)
  other arithmetic  1.88 us (3%)
    pallas_call x1, Pallas kernels, body(): pl.pallas_call(functools.partial(layer_kernel, pools, groups, experts), o...  55.5 us
    dot_general x1, matrix products, attend(): jnp.einsum('rqd,rcd->rqc', queries, cached_keys, preferred_element_type=j...  3.46 us
    unnamed x13, local copies, waits for them, and re-layouts  3.42 us

profile of v1, /device:TPU:0, one launch (start us, length us, event | category | flops | bytes accessed | tf_op | source)
XLA Modules:
  0.0 65.3 jit_solution(2620550542807697261)
XLA Ops:
  0.0 0.0 copy-start
  0.0 0.0 copy-start.2
  0.0 0.0 copy-start.1
  0.0 0.9 %iota_compare_fusion.1 = pred[32,512]{1,0:T(8,128)(4,1)S(1)} fusion(s32[32]{0:T(128)} %param.20), kind=kLoop, calls=%fused_computation.18 | loop fusion | flops 16384 | bytes 16512 | tf_op jit(solution)/shard_map/lt | solution.py:27
  0.9 1.3 %copy.24 = bf16[4,8,8,128]{3,2,1,0:T(8,128)(2,1)S(1)} copy(bf16[4,8,8,128]{3,1,2,0:T(8,128)(2,1)} %bitcast.35) | data formatting | bytes 131072
  2.2 0.0 copy-start.3
  2.2 0.0 copy-start.4
  2.2 3.5 %fusion.30 = (f32[32,8]{1,0:T(8,128)S(1)}, f32[32,8,512]{2,1,0:T(8,128)S(1)}) fusion(bf16[32,8,128]{2,1,0:T(8,128)(2,1)S(1)} %bitcast.31, bf16[32,1,512,128]{3,2,1,0:T(8,128)(2,1)} %param.16, pred[32,512]{1,0:T(8,128)(4,1)S(1)} %iota_compare_fusion.1), kind=kOutput, calls=%fused_computation.33 | convolution fusion | flops 33947392 | bytes 4801536 | tf_op jit(solution)/shard_map/rqd,rcd->rqc/dot_general | solution.py:21
  5.6 0.0 copy-done
  5.7 0.2 fusion.23
  5.8 0.3 fusion.16
  6.1 0.0 copy-done.2
  6.1 0.0 copy-done.1
  6.2 0.7 %fusion.13 = bf16[32,8,128]{2,1,0:T(8,128)(2,1)S(1)} fusion(bf16[32,1,512,128]{3,2,1,0:T(8,128)(2,1)S(1)} %copy-done.1, f32[32,8,512]{2,1,0:T(8,128)S(1)} %get-tuple-element.10, f32[32,8]{1,0:T(8,128)S(1)} %get-tuple-element.6, f32[32,8]{1,0:T(8,128)S(1)} %multiply_maximum_fusion, pred[32,512]{1,0:T(8,128)(4,1)S(1)} %iota_compare_fusion.1, ...), kind=kOutput, calls=%fused_computation.7 | convolution fusion | flops 34177024 | bytes 4819968 | tf_op jit(solution)/shard_map/rqc,rcd->rqd/dot_general | solution.py:35
  6.9 0.7 copy.29
  7.5 0.0 copy-done.3
  7.5 0.0 copy-done.4
  7.6 0.1 copy.19
  7.6 0.1 copy.20
  7.7 0.7 %fusion.26.gates_ref = bf16[32,128]{1,0:T(8,128)(2,1)} fusion(bf16[32,16]{1,0:T(8,128)(2,1)S(1)} %get-tuple-element.8, bf16[32,16]{1,0:T(8,128)(2,1)S(1)} %get-tuple-element.7), kind=kLoop, calls=%fused_computation.29 | loop fusion | flops 28672 | bytes 10240 | tf_op jit(solution)/shard_map/concatenate | solution.py:290
  8.4 55.5 %shard_map.136 = bf16[32,1024]{1,0:T(8,128)(2,1)} custom-call(bf16[32,1024]{1,0:T(8,128)(2,1)} %bitcast.29, bf16[32,4096]{1,0:T(8,128)(2,1)} %x_ref.1, bf16[32,128]{1,0:T(8,128)(2,1)} %fusion.26.gates_ref, f32[4,1,1024]{2,1,0:T(1,128)} %bitcast.36, bf16[1024,4096]{1,0:T(8,128)(2,1)} %proj_hbm.1, bf16[2,4096,256]{2,1,0:T(8,128)(2,1)} %gate_hbm.1, ...), custom_call_target="tpu_custom_call" | custom-call | tf_op jit(solution)/shard_map/pallas_call | solution.py:324
  63.9 1.5 %copy.31 = bf16[32,1024]{1,0:T(8,128)(2,1)} copy(bf16[32,1024]{1,0:T(8,128)(2,1)} %shard_map.136) | data formatting | bytes 131072
  (6 shorter events, 0.1 us)
Async XLA Ops:
  0.0 5.7 %copy-start = (bf16[32,128]{1,0:T(8,128)(2,1)S(1)}, bf16[32,128]{1,0:T(8,128)(2,1)}, u32[]{:S(2)}) copy-start(bf16[32,128]{1,0:T(8,128)(2,1)} %param.18) | copy-start | bytes 24580
  0.0 6.1 %copy-start.2 = (bf16[32,128]{1,0:T(8,128)(2,1)S(1)}, bf16[32,128]{1,0:T(8,128)(2,1)}, u32[]{:S(2)}) copy-start(bf16[32,128]{1,0:T(8,128)(2,1)} %param.19) | copy-start | bytes 24580
  0.0 6.1 %copy-start.1 = (bf16[32,1,512,128]{3,2,1,0:T(8,128)(2,1)S(1)}, bf16[32,1,512,128]{3,2,1,0:T(8,128)(2,1)}, u32[]{:S(2)}) copy-start(bf16[32,1,512,128]{3,2,1,0:T(8,128)(2,1)} %param.17) | copy-start | bytes 12582916
  2.2 5.4 %copy-start.3 = (f32[32,8]{0,1:T(8,128)S(1)}, f32[32,8]{0,1:T(8,128)}, u32[]{:S(2)}) copy-start(f32[32,8]{0,1:T(8,128)} %param.24) | copy-start | bytes 3076
  2.2 5.4 %copy-start.4 = (s32[32,8]{0,1:T(8,128)S(1)}, s32[32,8]{0,1:T(8,128)}, u32[]{:S(2)}) copy-start(s32[32,8]{0,1:T(8,128)} %param.23) | copy-start | bytes 3076

commit v2 on v1

v2 whole, which is shorter than its diff:
```python
import functools

import jax
import jax.numpy as jnp
from jax import lax
from jax.experimental import pallas as pl
from jax.experimental.pallas import tpu as pltpu
from jax.sharding import PartitionSpec as P

VMEM_BYTES = 60 * 1024 * 1024
HALVES = 2
TOGETHER = 8

MESH = pl.DeviceIdType.MESH
F32 = jnp.float32
BF16 = jnp.bfloat16


def flip(index, offset, count):
    result, bit = 0, 1
    while bit < count:
        result = result + bit * ((index // bit + offset // bit) % 2)
        bit *= 2
    return result


def layer_kernel(
    pools,
    groups,
    experts,
    lengths_ref,
    query_ref,
    new_key_ref,
    new_value_ref,
    x_ref,
    ids_ref,
    gate_weight_ref,
    gain_ref,
    key_hbm,
    value_hbm,
    proj_hbm,
    gate_hbm,
    up_hbm,
    down_hbm,
    out_ref,
    keys,
    values,
    query_heads,
    mixed_heads,
    fresh_keys,
    fresh_values,
    attn,
    proj,
    gate,
    up,
    down,
    part_send,
    part_recv,
    hidden,
    slabs,
    rows_all,
    act,
    produced,
    pair_recv,
    plane_recv,
    last_send,
    last_recv,
    cache_sem,
    load_sem,
    part_sems,
    slab_sems,
    gather_sems,
    pair_sems,
    swap_sems,
    plane_sems,
    last_sems,
):
    chips = pools // 2
    half, share = hidden.shape[1:]
    width = groups * share
    local = gate.shape[0]
    units = gate.shape[3]
    lanes = rows_all.shape[3] - width
    heads, head_size = query_heads.shape[1:]
    slots = keys.shape[1]
    pool, head = lax.axis_index("pool"), lax.axis_index("head")
    chip, core = pool // 2, pool % 2
    partner = {"pool": chip * 2 + 1 - core}
    above = [{"head": (head + k) % groups} for k in range(groups)]
    across = [{"pool": flip(chip, q, chips) * 2 + core} for q in range(chips)]
    order = list(range(1, groups)) + [0]
    sent = []

    def send(source, target, sems, place, device):
        copy = pltpu.make_async_remote_copy(
            src_ref=source,
            dst_ref=target,
            send_sem=sems.at[(0,) + place],
            recv_sem=sems.at[(1,) + place],
            device_id=device,
            device_id_type=MESH,
        )
        copy.start()
        sent.append(copy)
        return copy

    loads = {}

    def load(name, index, source, target):
        copy = pltpu.make_async_copy(source, target, load_sem.at[len(loads)])
        copy.start()
        loads[name, index] = copy

    def columns(k):
        return pl.ds(pl.multiple_of((head + k) % groups * share, share), share)

    def depths(k):
        return pl.ds(pl.multiple_of((head - k + groups) % groups * share, share), share)

    def cache_copies(index):
        place = pl.ds(index * TOGETHER, TOGETHER)
        return [
            pltpu.make_async_copy(key_hbm.at[place, 0], keys.at[place], cache_sem.at[0, index]),
            pltpu.make_async_copy(
                value_hbm.at[place, 0], values.at[place], cache_sem.at[1, index]
            ),
        ]

    blocks = half // TOGETHER

    def load_cache(a):
        for index in range(a * blocks, (a + 1) * blocks):
            for copy in cache_copies(index):
                copy.start()

    load_cache(0)
    for k in order:
        load("proj", k, proj_hbm.at[:, columns(k)], proj.at[k])
    for a in range(1, HALVES):
        load_cache(a)
    for k in range(groups):
        for e in range(local):
            load("gate", (e, k), gate_hbm.at[e, depths(k)], gate.at[e, k])
            load("up", (e, k), up_hbm.at[e, depths(k)], up.at[e, k])
    for k in order:
        for e in range(local):
            load("down", (e, k), down_hbm.at[e, :, columns(k)], down.at[k, e])

    barrier = pltpu.get_barrier_semaphore()
    greeted = above[1:] + across[1:] + [partner]
    for device in greeted:
        pl.semaphore_signal(barrier, inc=1, device_id=device, device_id_type=MESH)

    for i in range(heads):
        query_heads[:, i, :] = query_ref[:, i * head_size : (i + 1) * head_size].astype(F32)
    fresh_keys[...] = new_key_ref[...].astype(F32)
    fresh_values[...] = new_value_ref[...].astype(F32)
    score_scale = head_size ** (-0.5)

    def attend(a):
        def requests(index, carry):
            for copy in cache_copies(index):
                copy.wait()
            place = lax.broadcasted_iota(jnp.int32, (heads, slots), 1)
            for i in range(TOGETHER):
                r = index * TOGETHER + i
                queries = query_heads[r]
                scores = lax.dot_general(
                    queries.astype(BF16),
                    keys[r],
                    (((1,), (1,)), ((), ())),
                    preferred_element_type=F32,
                )
                scores = jnp.where(place < lengths_ref[r], scores * score_scale, -1e30)
                fresh = jnp.sum(queries * fresh_keys[pl.ds(r, 1)], -1, keepdims=True)
                fresh = fresh * score_scale
                highest = jnp.maximum(jnp.max(scores, -1, keepdims=True), fresh)
                weights = jnp.exp(scores - highest)
                own = jnp.exp(fresh - highest)
                total = jnp.sum(weights, -1, keepdims=True) + own
                mixed = jnp.dot(weights.astype(BF16), values[r], preferred_element_type=F32)
                mixed = mixed + own * fresh_values[pl.ds(r, 1)]
                mixed_heads[r] = mixed / total
            return carry

        lax.fori_loop(a * blocks, (a + 1) * blocks, requests, 0)
        place = slice(a * half, (a + 1) * half)
        for i in range(heads):
            attn[a, :, i * head_size : (i + 1) * head_size] = mixed_heads[place, i, :].astype(BF16)

    parts, shared, gathers, pairs, swaps, planes, lasts = {}, {}, {}, {}, {}, {}, {}

    def project_out(a):
        for k in order:
            if a == 0:
                loads["proj", k].wait()
            term = jnp.dot(attn[a], proj[k], preferred_element_type=F32)
            if k:
                part_send[a, k] = term.astype(BF16)
                parts[a, k] = send(
                    part_send.at[a, k], part_recv.at[a, k], part_sems, (a, k), above[k]
                )
            else:
                own = pl.ds(pl.multiple_of(head * share, share), share)
                hidden[a] = term + x_ref[a * half : (a + 1) * half, own].astype(F32)

    def share_hidden(a):
        total = hidden[a]
        for k in order[:-1]:
            parts[a, k].wait_recv()
            total = total + part_recv[a, k].astype(F32)
        hidden[a] = total
        slabs[a, 0] = total.astype(BF16)
        for k in order[:-1]:
            shared[a, k] = send(slabs.at[a, 0], slabs.at[a, k], slab_sems, (a, k), above[k])

    def gate_table(a):
        place = slice(a * half, (a + 1) * half)
        lane = lax.broadcasted_iota(jnp.int32, (half, lanes), 1)
        expert = jnp.where(lane < experts, lane, lane - experts)
        ids, weights = ids_ref[place, :], gate_weight_ref[place, :]
        table = jnp.zeros((half, lanes), F32)
        for i in range(ids.shape[1]):
            table += jnp.where(ids[:, i : i + 1] == expert, weights[:, i : i + 1], 0.0)
        first = table.astype(BF16).astype(F32)
        return jnp.where(lane < experts, first, table - first).astype(BF16)

    def norm_and_gather(a):
        rows_all[a, 0, :, width:] = gate_table(a)
        for k in order[:-1]:
            shared[a, k].wait_recv()
        squares = jnp.zeros((half, 1), F32)
        for k in range(groups):
            value = slabs[a, k].astype(F32)
            squares = squares + jnp.sum(value * value, -1, keepdims=True)
        scale = lax.rsqrt(squares / width + 1e-06)
        for k in range(groups):
            slab_gain = gain_ref[(head - k + groups) % groups]
            rows_all[a, 0, :, k * share : (k + 1) * share] = (
                slabs[a, k].astype(F32) * scale * slab_gain
            ).astype(BF16)
        for q in range(1, chips):
            gathers[a, q] = send(
                rows_all.at[a, 0], rows_all.at[a, q], gather_sems, (a, q), across[q]
            )
        pairs[a, 0] = send(
            rows_all.at[a, 0], rows_all.at[a, chips], pair_sems, (a, 0), partner
        )

    def pass_to_partner(a):
        for q in range(1, chips):
            gathers[a, q].wait_recv()
            pairs[a, q] = send(
                rows_all.at[a, q], rows_all.at[a, chips + q], pair_sems, (a, q), partner
            )
        for q in range(chips):
            pairs[a, q].wait_recv()

    block = min(16, pools)

    def expert_rows(a):
        if a == 0:
            for k in range(groups):
                for e in range(local):
                    loads["gate", (e, k)].wait()
                    loads["up", (e, k)].wait()

        def some_rows(index, carry):
            place = pl.ds(index * block, block)
            gates = rows_all[a, place, :, width:].reshape(block * half, -1).astype(F32)
            lane = lax.broadcasted_iota(jnp.int32, gates.shape, 1)
            for e in range(local):
                gate_part = jnp.zeros((block * half, units), F32)
                up_part = jnp.zeros((block * half, units), F32)
                for k in range(groups):
                    piece = rows_all[a, place, :, k * share : (k + 1) * share].reshape(
                        block * half, share
                    )
                    gate_part += jnp.dot(piece, gate[e, k], preferred_element_type=F32)
                    up_part += jnp.dot(piece, up[e, k], preferred_element_type=F32)
                expert = pool * local + e
                chosen = (lane == expert) | (lane == experts + expert)
                weight = jnp.sum(jnp.where(chosen, gates, 0.0), -1, keepdims=True)
                value = gate_part / (1.0 + jnp.exp(-gate_part)) * up_part * weight
                act[place, :, e * units : (e + 1) * units] = value.astype(BF16).reshape(
                    block, half, units
                )
            return carry

        lax.fori_loop(0, pools // block, some_rows, 0)

    def project_down(a, k):
        if a == 0:
            for e in range(local):
                loads["down", (e, k)].wait()

        def some_rows(index, carry):
            place = pl.ds(index * block, block)
            value = jnp.dot(
                act[place].reshape(block * half, local * units),
                down[k].reshape(local * units, share),
                preferred_element_type=F32,
            )
            produced[a, k, place] = value.astype(BF16).reshape(block, half, share)
            return carry

        lax.fori_loop(0, pools // block, some_rows, 0)
        swaps[a, k] = send(
            produced.at[a, k, pl.ds(chips, chips)],
            pair_recv.at[a, k],
            swap_sems,
            (a, k),
            partner,
        )

    def cross(a, k):
        swaps[a, k].wait_recv()
        for q in range(1, chips):
            produced[a, k, q] = (
                produced[a, k, q].astype(F32) + pair_recv[a, k, q].astype(F32)
            ).astype(BF16)
            planes[a, k, q] = send(
                produced.at[a, k, q],
                plane_recv.at[a, k, q],
                plane_sems,
                (a, k, q),
                across[q],
            )

    def finish(a, k):
        value = produced[a, k, 0].astype(F32) + pair_recv[a, k, 0].astype(F32)
        for q in range(1, chips):
            planes[a, k, q].wait_recv()
            value = value + plane_recv[a, k, q].astype(F32)
        if k:
            last_send[a, k] = value.astype(BF16)
            lasts[a, k] = send(
                last_send.at[a, k], last_recv.at[a, k], last_sems, (a, k), above[k]
            )
        else:
            hidden[a] = hidden[a] + value

    def write(a):
        value = hidden[a]
        for k in order[:-1]:
            lasts[a, k].wait_recv()
            value = value + last_recv[a, k].astype(F32)
        out_ref[a * half : (a + 1) * half, :] = value

    def experts_out(a, between):
        expert_rows(a)
        for step in range(groups + 1):
            if step < groups:
                project_down(a, order[step])
            if step:
                cross(a, order[step - 1])
                between(order[step - 1])

    attend(0)
    pl.semaphore_wait(barrier, len(greeted))
    project_out(0)
    attend(1)
    share_hidden(0)
    project_out(1)
    norm_and_gather(0)
    share_hidden(1)
    norm_and_gather(1)
    pass_to_partner(0)
    experts_out(0, lambda k: None)
    pass_to_partner(1)
    experts_out(1, lambda k: finish(0, k))
    for k in order:
        finish(1, k)
    write(0)
    write(1)
    for copy in sent:
        copy.wait_send()


def body(
    x_rows,
    query,
    key_cache,
    value_cache,
    new_key,
    new_value,
    lengths,
    out_proj,
    norm_gain,
    expert_ids,
    gate_weights,
    w_gate,
    w_up,
    w_down,
):
    pools = lax.axis_size("pool")
    groups = lax.axis_size("head")
    rows, width = x_rows.shape
    share = width // groups
    local, _, units = w_gate.shape
    experts = pools * local
    chips = pools // 2
    half = rows // HALVES
    head_size = new_key.shape[1]
    heads = query.shape[1] // head_size
    slots = key_cache.shape[2]
    lanes = -(-2 * experts // 128) * 128
    depth = out_proj.shape[0]
    in_smem = pl.BlockSpec(memory_space=pltpu.SMEM)
    in_vmem = pl.BlockSpec(memory_space=pltpu.VMEM)
    in_hbm = pl.BlockSpec(memory_space=pl.ANY)
    dma = pltpu.SemaphoreType.DMA
    summed = pl.pallas_call(
        functools.partial(layer_kernel, pools, groups, experts),
        out_shape=jax.ShapeDtypeStruct((rows, share), F32),
        in_specs=[in_smem] + [in_vmem] * 7 + [in_hbm] * 6,
        out_specs=in_vmem,
        scratch_shapes=[
            pltpu.VMEM((rows, slots, head_size), BF16),
            pltpu.VMEM((rows, slots, head_size), BF16),
            pltpu.VMEM((rows, heads, head_size), F32),
            pltpu.VMEM((rows, heads, head_size), F32),
            pltpu.VMEM((rows, head_size), F32),
            pltpu.VMEM((rows, head_size), F32),
            pltpu.VMEM((HALVES, half, depth), BF16),
            pltpu.VMEM((groups, depth, share), BF16),
            pltpu.VMEM((local, groups, share, units), BF16),
            pltpu.VMEM((local, groups, share, units), BF16),
            pltpu.VMEM((groups, local, units, share), BF16),
            pltpu.VMEM((HALVES, groups, half, share), BF16),
            pltpu.VMEM((HALVES, groups, half, share), BF16),
            pltpu.VMEM((HALVES, half, share), F32),
            pltpu.VMEM((HALVES, groups, half, share), BF16),
            pltpu.VMEM((HALVES, pools, half, width + lanes), BF16),
            pltpu.VMEM((pools, half, local * units), BF16),
            pltpu.VMEM((HALVES, groups, pools, half, share), BF16),
            pltpu.VMEM((HALVES, groups, chips, half, share), BF16),
            pltpu.VMEM((HALVES, groups, chips, half, share), BF16),
            pltpu.VMEM((HALVES, groups, half, share), BF16),
            pltpu.VMEM((HALVES, groups, half, share), BF16),
            dma((2, rows // TOGETHER)),
            dma((groups * (1 + 3 * local),)),
            dma((2, HALVES, groups)),
            dma((2, HALVES, groups)),
            dma((2, HALVES, chips)),
            dma((2, HALVES, chips)),
            dma((2, HALVES, groups)),
            dma((2, HALVES, groups, chips)),
            dma((2, HALVES, groups)),
        ],
        compiler_params=pltpu.CompilerParams(
            collective_id=0, has_side_effects=True, vmem_limit_bytes=VMEM_BYTES
        ),
    )(
        lengths,
        query,
        new_key,
        new_value,
        x_rows,
        expert_ids,
        gate_weights,
        norm_gain.reshape(groups, 1, share),
        key_cache,
        value_cache,
        out_proj,
        w_gate,
        w_up,
        w_down,
    )
    return summed.astype(BF16)


def solution(mesh):
    placed = (
        P("pool", None),
        P("pool", "head"),
        P("pool", "head", None, None),
        P("pool", "head", None, None),
        P("pool", "head"),
        P("pool", "head"),
        P("pool"),
        P("head", None),
        P(),
        P("pool", None),
        P("pool", None),
        P("pool", None, "head"),
        P("pool", None, "head"),
        P("pool", "head", None),
    )
    return jax.shard_map(
        body, mesh=mesh, in_specs=placed, out_specs=P("pool", "head"), check_vma=False
    )
```

time: 65.5 us -> 60.1 us (0.918)
  matrix products: 4.35 us -> 0 us
  local copies, waits for them, and re-layouts: 3.56 us -> 2.72 us
    dot_general x3 -> x0, matrix products: 4.35 us -> none  [the longest x1 3.46 us: attend(): jnp.einsum('rqd,rcd->rqc', queries, cached_keys, preferred_element_type=j...]
    convert_element_type x2 -> x1, other arithmetic: 0.02 us -> 1.54 us  [body(): return summed.astype(BF16)]
    lt x1 -> x0, other arithmetic: 0.88 us -> none  [attend(): jnp.arange(cached_keys.shape[1])[None, :] < lengths[:, None]]
    unnamed x13 -> x2, local copies, waits for them, and re-layouts: 3.42 us -> 2.72 us
    concatenate x1 -> x0, other arithmetic: 0.68 us -> none  [gate_table(): both = jnp.concatenate([first, rest], 1).astype(BF16)]
where the time goes in v2:
time: 60.1 us; the launch traced here: 59.9 us
  Pallas kernels  55.6 us (93%)
  local copies, waits for them, and re-layouts  2.72 us (5%)
  other arithmetic  1.54 us (3%)
    pallas_call x1, Pallas kernels, body(): pl.pallas_call(functools.partial(layer_kernel, pools, groups, experts), o...  55.6 us
    unnamed x2, local copies, waits for them, and re-layouts  2.72 us
    convert_element_type x1, other arithmetic, body(): return summed.astype(BF16)  1.54 us

profile of v2, /device:TPU:0, one launch (start us, length us, event | category | flops | bytes accessed | tf_op | source)
XLA Modules:
  0.0 59.9 jit_solution(6551048200144453318)
XLA Ops:
  0.0 1.4 %copy.15.ids_ref = s32[32,8]{1,0:T(8,128)} copy(s32[32,8]{0,1:T(8,128)} %param.23) | data formatting | bytes 2048 | tf_op args[9]
  1.4 1.4 %copy.16.gate_weight_ref = f32[32,8]{1,0:T(8,128)} copy(f32[32,8]{0,1:T(8,128)} %param.24) | data formatting | bytes 2048 | tf_op args[10]
  2.7 55.6 %shard_map.136 = f32[32,1024]{1,0:T(8,128)} custom-call(s32[32]{0:T(128)} %lengths_ref.1, bf16[32,1024]{1,0:T(8,128)(2,1)} %query_ref.1, bf16[32,128]{1,0:T(8,128)(2,1)} %new_key_ref.1, bf16[32,128]{1,0:T(8,128)(2,1)} %new_value_ref.1, bf16[32,4096]{1,0:T(8,128)(2,1)} %x_ref.1, s32[32,8]{1,0:T(8,128)} %copy.15.ids_ref, f32[32,8]{1,0:T(8,128)} %copy.16.gate_weight_ref, ...), custom_call_target="tpu_custom_call" | custom-call | tf_op jit(solution)/shard_map/pallas_call | solution.py:413
  58.3 1.5 %convert_element_type.3 = bf16[32,1024]{1,0:T(8,128)(2,1)} convert(f32[32,1024]{1,0:T(8,128)} %shard_map.136) | non-fusion elementwise | flops 32768 | bytes 196608 | tf_op jit(solution)/shard_map/convert_element_type | solution.py:470

commit v3 on v2

--- a/solution.py
+++ b/solution.py
@@ -63,6 +63,10 @@
     produced,
     pair_recv,
     plane_recv,
+    first_send,
+    first_recv,
+    second_send,
+    second_recv,
     last_send,
     last_recv,
     cache_sem,
@@ -90,6 +94,9 @@
     across = [{"pool": flip(chip, q, chips) * 2 + core} for q in range(chips)]
     order = list(range(1, groups)) + [0]
     sent = []
+    relayed = chips == 4
+    cuts = [pl.ds(0, width // 2), pl.ds(width // 2, width - width // 2 + lanes)]
+    sides = [slice(0, share // 2), slice(share // 2, share)]
 
     def send(source, target, sems, place, device):
         copy = pltpu.make_async_remote_copy(
@@ -156,6 +163,22 @@
     fresh_keys[...] = new_key_ref[...].astype(F32)
     fresh_values[...] = new_value_ref[...].astype(F32)
     score_scale = head_size ** (-0.5)
+
+    rows = HALVES * half
+    lane = lax.broadcasted_iota(jnp.int32, (lanes, rows), 0)
+    named = jnp.where(lane < experts, lane, lane - experts)
+    table = jnp.zeros((lanes, rows), F32)
+    for i in range(ids_ref.shape[0]):
+        table += jnp.where(ids_ref[i : i + 1, :] == named, gate_weight_ref[i : i + 1, :], 0.0)
+    first = table.astype(BF16).astype(F32)
+    terms = jnp.where(lane < experts, first, table - first).astype(BF16)
+    square = (rows, rows)
+    eye = lax.broadcasted_iota(jnp.int32, square, 0) == lax.broadcasted_iota(jnp.int32, square, 1)
+    terms = lax.dot_general(
+        eye.astype(F32).astype(BF16), terms, (((1,), (1,)), ((), ())), preferred_element_type=F32
+    ).astype(BF16)
+    for a in range(HALVES):
+        rows_all[a, 0, :, width:] = terms[a * half : (a + 1) * half]
 
     def attend(a):
         def requests(index, carry):
@@ -214,19 +237,7 @@
         for k in order[:-1]:
             shared[a, k] = send(slabs.at[a, 0], slabs.at[a, k], slab_sems, (a, k), above[k])
 
-    def gate_table(a):
-        place = slice(a * half, (a + 1) * half)
-        lane = lax.broadcasted_iota(jnp.int32, (half, lanes), 1)
-        expert = jnp.where(lane < experts, lane, lane - experts)
-        ids, weights = ids_ref[place, :], gate_weight_ref[place, :]
-        table = jnp.zeros((half, lanes), F32)
-        for i in range(ids.shape[1]):
-            table += jnp.where(ids[:, i : i + 1] == expert, weights[:, i : i + 1], 0.0)
-        first = table.astype(BF16).astype(F32)
-        return jnp.where(lane < experts, first, table - first).astype(BF16)
-
     def norm_and_gather(a):
-        rows_all[a, 0, :, width:] = gate_table(a)
         for k in order[:-1]:
             shared[a, k].wait_recv()
         squares = jnp.zeros((half, 1), F32)
@@ -239,17 +250,45 @@
             rows_all[a, 0, :, k * share : (k + 1) * share] = (
                 slabs[a, k].astype(F32) * scale * slab_gain
             ).astype(BF16)
-        for q in range(1, chips):
-            gathers[a, q] = send(
-                rows_all.at[a, 0], rows_all.at[a, q], gather_sems, (a, q), across[q]
-            )
         pairs[a, 0] = send(
             rows_all.at[a, 0], rows_all.at[a, chips], pair_sems, (a, 0), partner
         )
+        if relayed:
+            for q, c in ((1, 0), (2, 1), (1, 1), (2, 0)):
+                gathers[a, q, c] = send(
+                    rows_all.at[a, 0, :, cuts[c]],
+                    rows_all.at[a, q, :, cuts[c]],
+                    gather_sems,
+                    (a, q, c),
+                    across[q],
+                )
+        else:
+            for q in range(1, chips):
+                gathers[a, q] = send(
+                    rows_all.at[a, 0], rows_all.at[a, q], gather_sems, (a, q, 0), across[q]
+                )
+
+    def relay(a):
+        if relayed:
+            for c, near, far in ((0, 1, 2), (1, 2, 1)):
+                gathers[a, near, c].wait_recv()
+                gathers[a, 3, c] = send(
+                    rows_all.at[a, near, :, cuts[c]],
+                    rows_all.at[a, 3, :, cuts[c]],
+                    gather_sems,
+                    (a, 3, c),
+                    across[far],
+                )
 
     def pass_to_partner(a):
         for q in range(1, chips):
-            gathers[a, q].wait_recv()
+            if not relayed:
+                gathers[a, q].wait_recv()
+            elif q < 3:
+                gathers[a, q, 2 - q].wait_recv()
+            else:
+                gathers[a, q, 0].wait_recv()
+                gathers[a, q, 1].wait_recv()
             pairs[a, q] = send(
                 rows_all.at[a, q], rows_all.at[a, chips + q], pair_sems, (a, q), partner
             )
@@ -313,25 +352,61 @@
             partner,
         )
 
+    def summed(a, k, q, side=slice(None)):
+        return produced[a, k, q, :, side].astype(F32) + pair_recv[a, k, q, :, side].astype(F32)
+
     def cross(a, k):
         swaps[a, k].wait_recv()
-        for q in range(1, chips):
-            produced[a, k, q] = (
-                produced[a, k, q].astype(F32) + pair_recv[a, k, q].astype(F32)
-            ).astype(BF16)
-            planes[a, k, q] = send(
-                produced.at[a, k, q],
-                plane_recv.at[a, k, q],
-                plane_sems,
-                (a, k, q),
-                across[q],
-            )
+        if relayed:
+            for d in range(2):
+                first_send[a, k, d, 0] = summed(a, k, 1 + d, sides[d]).astype(BF16)
+                first_send[a, k, d, 1] = summed(a, k, 3, sides[d]).astype(BF16)
+                planes[a, k, d] = send(
+                    first_send.at[a, k, d],
+                    first_recv.at[a, k, d],
+                    plane_sems,
+                    (a, k, d),
+                    across[1 + d],
+                )
+        else:
+            for q in range(1, chips):
+                produced[a, k, q] = summed(a, k, q).astype(BF16)
+                planes[a, k, q] = send(
+                    produced.at[a, k, q],
+                    plane_recv.at[a, k, q],
+                    plane_sems,
+                    (a, k, q),
+                    across[q],
+                )
+
+    def cross_again(a, k):
+        if relayed:
+            for d in range(2):
+                planes[a, k, d].wait_recv()
+                value = summed(a, k, 2 - d, sides[d]) + first_recv[a, k, d, 1].astype(F32)
+                second_send[a, k, d] = value.astype(BF16)
+                planes[a, k, 2 + d] = send(
+                    second_send.at[a, k, d],
+                    second_recv.at[a, k, d],
+                    plane_sems,
+                    (a, k, 2 + d),
+                    across[2 - d],
+                )
 
     def finish(a, k):
-        value = produced[a, k, 0].astype(F32) + pair_recv[a, k, 0].astype(F32)
-        for q in range(1, chips):
-            planes[a, k, q].wait_recv()
-            value = value + plane_recv[a, k, q].astype(F32)
+        value = summed(a, k, 0)
+        if relayed:
+            planes[a, k, 2].wait_recv()
+            planes[a, k, 3].wait_recv()
+            came = [
+                first_recv[a, k, d, 0].astype(F32) + second_recv[a, k, d].astype(F32)
+                for d in range(2)
+            ]
+            value = value + jnp.concatenate(came, 1)
+        else:
+            for q in range(1, chips):
+                planes[a, k, q].wait_recv()
+                value = value + plane_recv[a, k, q].astype(F32)
         if k:
             last_send[a, k] = value.astype(BF16)
             lasts[a, k] = send(
@@ -347,14 +422,15 @@
             value = value + last_recv[a, k].astype(F32)
         out_ref[a * half : (a + 1) * half, :] = value
 
-    def experts_out(a, between):
-        expert_rows(a)
-        for step in range(groups + 1):
+    def down_out(a, between):
+        for step in range(groups + 2):
             if step < groups:
                 project_down(a, order[step])
-            if step:
+            if 1 <= step <= groups:
                 cross(a, order[step - 1])
                 between(order[step - 1])
+            if step >= 2:
+                cross_again(a, order[step - 2])
 
     attend(0)
     pl.semaphore_wait(barrier, len(greeted))
@@ -364,11 +440,15 @@
     project_out(1)
     norm_and_gather(0)
     share_hidden(1)
+    relay(0)
     norm_and_gather(1)
     pass_to_partner(0)
-    experts_out(0, lambda k: None)
+    expert_rows(0)
+    relay(1)
+    down_out(0, lambda k: None)
     pass_to_partner(1)
-    experts_out(1, lambda k: finish(0, k))
+    expert_rows(1)
+    down_out(1, lambda k: finish(0, k))
     for k in order:
         finish(1, k)
     write(0)
@@ -406,6 +486,9 @@
     slots = key_cache.shape[2]
     lanes = -(-2 * experts // 128) * 128
     depth = out_proj.shape[0]
+    relayed = chips == 4
+    first = (HALVES, groups, 2, 2, half, share // 2) if relayed else (1,) * 6
+    second = (HALVES, groups, 2, half, share // 2) if relayed else (1,) * 5
     in_smem = pl.BlockSpec(memory_space=pltpu.SMEM)
     in_vmem = pl.BlockSpec(memory_space=pltpu.VMEM)
     in_hbm = pl.BlockSpec(memory_space=pl.ANY)
@@ -435,14 +518,18 @@
             pltpu.VMEM((pools, half, local * units), BF16),
             pltpu.VMEM((HALVES, groups, pools, half, share), BF16),
             pltpu.VMEM((HALVES, groups, chips, half, share), BF16),
-            pltpu.VMEM((HALVES, groups, chips, half, share), BF16),
+            pltpu.VMEM((1,) * 5 if relayed else (HALVES, groups, chips, half, share), BF16),
+            pltpu.VMEM(first, BF16),
+            pltpu.VMEM(first, BF16),
+            pltpu.VMEM(second, BF16),
+            pltpu.VMEM(second, BF16),
             pltpu.VMEM((HALVES, groups, half, share), BF16),
             pltpu.VMEM((HALVES, groups, half, share), BF16),
             dma((2, rows // TOGETHER)),
             dma((groups * (1 + 3 * local),)),
             dma((2, HALVES, groups)),
             dma((2, HALVES, groups)),
-            dma((2, HALVES, chips)),
+            dma((2, HALVES, chips, 2)),
             dma((2, HALVES, chips)),
             dma((2, HALVES, groups)),
             dma((2, HALVES, groups, chips)),
@@ -457,8 +544,8 @@
         new_key,
         new_value,
         x_rows,
-        expert_ids,
-        gate_weights,
+        expert_ids.T,
+        gate_weights.T,
         norm_gain.reshape(groups, 1, share),
         key_cache,
         value_cache,

time: 60.1 us -> 65.9 us (1.097)
  Pallas kernels: 55.6 us -> 64.1 us
  local copies, waits for them, and re-layouts: 2.72 us -> 0 us
    pallas_call x1, Pallas kernels: 55.6 us -> 64.1 us  [body(): pl.pallas_call(functools.partial(layer_kernel, pools, groups, experts), o...]
    unnamed x2 -> x0, local copies, waits for them, and re-layouts: 2.72 us -> none
where the time goes in v3:
time: 65.9 us; the launch traced here: 65.7 us
  Pallas kernels  64.1 us (97%)
  other arithmetic  1.54 us (2%)
    pallas_call x1, Pallas kernels, body(): pl.pallas_call(functools.partial(layer_kernel, pools, groups, experts), o...  64.1 us
    convert_element_type x1, other arithmetic, body(): return summed.astype(BF16)  1.54 us

profile of v3, /device:TPU:0, one launch (start us, length us, event | category | flops | bytes accessed | tf_op | source)
XLA Modules:
  0.0 65.7 jit_solution(16035792866295971051)
XLA Ops:
  0.0 64.1 %shard_map.136 = f32[32,1024]{1,0:T(8,128)} custom-call(s32[32]{0:T(128)} %lengths_ref.1, bf16[32,1024]{1,0:T(8,128)(2,1)} %query_ref.1, bf16[32,128]{1,0:T(8,128)(2,1)} %new_key_ref.1, bf16[32,128]{1,0:T(8,128)(2,1)} %new_value_ref.1, bf16[32,4096]{1,0:T(8,128)(2,1)} %x_ref.1, s32[8,32]{1,0:T(8,128)} %bitcast.4, f32[8,32]{1,0:T(8,128)} %bitcast.5, ...), custom_call_target="tpu_custom_call" | custom-call | tf_op jit(solution)/shard_map/pallas_call | solution.py:496
  64.1 1.5 %convert_element_type.3 = bf16[32,1024]{1,0:T(8,128)(2,1)} convert(f32[32,1024]{1,0:T(8,128)} %shard_map.136) | non-fusion elementwise | flops 32768 | bytes 196608 | tf_op jit(solution)/shard_map/convert_element_type | solution.py:557

commit v4 on v2

--- a/solution.py
+++ b/solution.py
@@ -157,30 +157,65 @@
     fresh_values[...] = new_value_ref[...].astype(F32)
     score_scale = head_size ** (-0.5)
 
+    rows = HALVES * half
+    lane = lax.broadcasted_iota(jnp.int32, (lanes, rows), 0)
+    named = jnp.where(lane < experts, lane, lane - experts)
+    table = jnp.zeros((lanes, rows), F32)
+    for i in range(ids_ref.shape[0]):
+        table += jnp.where(ids_ref[i : i + 1, :] == named, gate_weight_ref[i : i + 1, :], 0.0)
+    first = table.astype(BF16).astype(F32)
+    terms = jnp.where(lane < experts, first, table - first).astype(BF16)
+    square = (rows, rows)
+    eye = lax.broadcasted_iota(jnp.int32, square, 0) == lax.broadcasted_iota(jnp.int32, square, 1)
+    terms = lax.dot_general(
+        eye.astype(F32).astype(BF16), terms, (((1,), (1,)), ((), ())), preferred_element_type=F32
+    ).astype(BF16)
+    for a in range(HALVES):
+        rows_all[a, 0, :, width:] = terms[a * half : (a + 1) * half]
+
     def attend(a):
         def requests(index, carry):
             for copy in cache_copies(index):
                 copy.wait()
             place = lax.broadcasted_iota(jnp.int32, (heads, slots), 1)
-            for i in range(TOGETHER):
-                r = index * TOGETHER + i
-                queries = query_heads[r]
-                scores = lax.dot_general(
-                    queries.astype(BF16),
+            numbers = [index * TOGETHER + i for i in range(TOGETHER)]
+            queries = [query_heads[r] for r in numbers]
+            scores = [
+                lax.dot_general(
+                    query.astype(BF16),
                     keys[r],
                     (((1,), (1,)), ((), ())),
                     preferred_element_type=F32,
                 )
-                scores = jnp.where(place < lengths_ref[r], scores * score_scale, -1e30)
-                fresh = jnp.sum(queries * fresh_keys[pl.ds(r, 1)], -1, keepdims=True)
-                fresh = fresh * score_scale
-                highest = jnp.maximum(jnp.max(scores, -1, keepdims=True), fresh)
-                weights = jnp.exp(scores - highest)
-                own = jnp.exp(fresh - highest)
-                total = jnp.sum(weights, -1, keepdims=True) + own
-                mixed = jnp.dot(weights.astype(BF16), values[r], preferred_element_type=F32)
-                mixed = mixed + own * fresh_values[pl.ds(r, 1)]
-                mixed_heads[r] = mixed / total
+                for r, query in zip(numbers, queries)
+            ]
+            scores = [
+                jnp.where(place < lengths_ref[r], score * score_scale, -1e30)
+                for r, score in zip(numbers, scores)
+            ]
+            fresh = [
+                jnp.sum(query * fresh_keys[pl.ds(r, 1)], -1, keepdims=True) * score_scale
+                for r, query in zip(numbers, queries)
+            ]
+            highest = [
+                jnp.maximum(jnp.max(score, -1, keepdims=True), new)
+                for score, new in zip(scores, fresh)
+            ]
+            weights = [jnp.exp(score - top) for score, top in zip(scores, highest)]
+            mixed = [
+                jnp.dot(weight.astype(BF16), values[r], preferred_element_type=F32)
+                for r, weight in zip(numbers, weights)
+            ]
+            own = [jnp.exp(new - top) for new, top in zip(fresh, highest)]
+            totals = [
+                jnp.sum(weight, -1, keepdims=True) + new for weight, new in zip(weights, own)
+            ]
+            mixed = [
+                (value + new * fresh_values[pl.ds(r, 1)]) / total
+                for r, value, new, total in zip(numbers, mixed, own, totals)
+            ]
+            for r, value in zip(numbers, mixed):
+                mixed_heads[r] = value
             return carry
 
         lax.fori_loop(a * blocks, (a + 1) * blocks, requests, 0)
@@ -214,19 +249,7 @@
         for k in order[:-1]:
             shared[a, k] = send(slabs.at[a, 0], slabs.at[a, k], slab_sems, (a, k), above[k])
 
-    def gate_table(a):
-        place = slice(a * half, (a + 1) * half)
-        lane = lax.broadcasted_iota(jnp.int32, (half, lanes), 1)
-        expert = jnp.where(lane < experts, lane, lane - experts)
-        ids, weights = ids_ref[place, :], gate_weight_ref[place, :]
-        table = jnp.zeros((half, lanes), F32)
-        for i in range(ids.shape[1]):
-            table += jnp.where(ids[:, i : i + 1] == expert, weights[:, i : i + 1], 0.0)
-        first = table.astype(BF16).astype(F32)
-        return jnp.where(lane < experts, first, table - first).astype(BF16)
-
     def norm_and_gather(a):
-        rows_all[a, 0, :, width:] = gate_table(a)
         for k in order[:-1]:
             shared[a, k].wait_recv()
         squares = jnp.zeros((half, 1), F32)
@@ -253,6 +276,8 @@
             pairs[a, q] = send(
                 rows_all.at[a, q], rows_all.at[a, chips + q], pair_sems, (a, q), partner
             )
+
+    def take_from_partner(a):
         for q in range(chips):
             pairs[a, q].wait_recv()
 
@@ -347,14 +372,16 @@
             value = value + last_recv[a, k].astype(F32)
         out_ref[a * half : (a + 1) * half, :] = value
 
-    def experts_out(a, between):
-        expert_rows(a)
+    def down_out(a, between):
         for step in range(groups + 1):
             if step < groups:
                 project_down(a, order[step])
+            else:
+                between(step)
             if step:
                 cross(a, order[step - 1])
-                between(order[step - 1])
+                if step < groups:
+                    between(step)
 
     attend(0)
     pl.semaphore_wait(barrier, len(greeted))
@@ -366,9 +393,12 @@
     share_hidden(1)
     norm_and_gather(1)
     pass_to_partner(0)
-    experts_out(0, lambda k: None)
-    pass_to_partner(1)
-    experts_out(1, lambda k: finish(0, k))
+    take_from_partner(0)
+    expert_rows(0)
+    down_out(0, lambda step: pass_to_partner(1) if step == groups else None)
+    take_from_partner(1)
+    expert_rows(1)
+    down_out(1, lambda step: finish(0, order[step - 1]))
     for k in order:
         finish(1, k)
     write(0)
@@ -457,8 +487,8 @@
         new_key,
         new_value,
         x_rows,
-        expert_ids,
-        gate_weights,
+        expert_ids.T,
+        gate_weights.T,
         norm_gain.reshape(groups, 1, share),
         key_cache,
         value_cache,

time: 60.1 us -> 53 us (0.88)
  Pallas kernels: 55.6 us -> 51.3 us
  local copies, waits for them, and re-layouts: 2.72 us -> 0 us
    pallas_call x1, Pallas kernels: 55.6 us -> 51.3 us  [body(): pl.pallas_call(functools.partial(layer_kernel, pools, groups, experts), o...]
    unnamed x2 -> x0, local copies, waits for them, and re-layouts: 2.72 us -> none
where the time goes in v4:
time: 53 us; the launch traced here: 52.8 us
  Pallas kernels  51.3 us (97%)
  other arithmetic  1.54 us (3%)
    pallas_call x1, Pallas kernels, body(): pl.pallas_call(functools.partial(layer_kernel, pools, groups, experts), o...  51.3 us
    convert_element_type x1, other arithmetic, body(): return summed.astype(BF16)  1.54 us

profile of v4, /device:TPU:0, one launch (start us, length us, event | category | flops | bytes accessed | tf_op | source)
XLA Modules:
  0.0 52.8 jit_solution(4165501098767141054)
XLA Ops:
  0.0 51.3 %shard_map.136 = f32[32,1024]{1,0:T(8,128)} custom-call(s32[32]{0:T(128)} %lengths_ref.1, bf16[32,1024]{1,0:T(8,128)(2,1)} %query_ref.1, bf16[32,128]{1,0:T(8,128)(2,1)} %new_key_ref.1, bf16[32,128]{1,0:T(8,128)(2,1)} %new_value_ref.1, bf16[32,4096]{1,0:T(8,128)(2,1)} %x_ref.1, s32[8,32]{1,0:T(8,128)} %bitcast.4, f32[8,32]{1,0:T(8,128)} %bitcast.5, ...), custom_call_target="tpu_custom_call" | custom-call | tf_op jit(solution)/shard_map/pallas_call | solution.py:443
  51.3 1.5 %convert_element_type.3 = bf16[32,1024]{1,0:T(8,128)(2,1)} convert(f32[32,1024]{1,0:T(8,128)} %shard_map.136) | non-fusion elementwise | flops 32768 | bytes 196608 | tf_op jit(solution)/shard_map/convert_element_type | solution.py:500

commit v5 on v4

--- a/solution.py
+++ b/solution.py
@@ -134,17 +134,21 @@
                 copy.start()
 
     load_cache(0)
-    for k in order:
-        load("proj", k, proj_hbm.at[:, columns(k)], proj.at[k])
-    for a in range(1, HALVES):
-        load_cache(a)
-    for k in range(groups):
-        for e in range(local):
-            load("gate", (e, k), gate_hbm.at[e, depths(k)], gate.at[e, k])
-            load("up", (e, k), up_hbm.at[e, depths(k)], up.at[e, k])
-    for k in order:
-        for e in range(local):
-            load("down", (e, k), down_hbm.at[e, :, columns(k)], down.at[k, e])
+
+    def load_projection():
+        for k in order:
+            load("proj", k, proj_hbm.at[:, columns(k)], proj.at[k])
+
+    def load_inward():
+        for k in range(groups):
+            for e in range(local):
+                load("gate", (e, k), gate_hbm.at[e, depths(k)], gate.at[e, k])
+                load("up", (e, k), up_hbm.at[e, depths(k)], up.at[e, k])
+
+    def load_down():
+        for k in order:
+            for e in range(local):
+                load("down", (e, k), down_hbm.at[e, :, columns(k)], down.at[k, e])
 
     barrier = pltpu.get_barrier_semaphore()
     greeted = above[1:] + across[1:] + [partner]
@@ -373,20 +377,25 @@
         out_ref[a * half : (a + 1) * half, :] = value
 
     def down_out(a, between):
-        for step in range(groups + 1):
+        for step in range(groups + 2):
             if step < groups:
                 project_down(a, order[step])
             else:
-                between(step)
-            if step:
-                cross(a, order[step - 1])
+                between(step - 2)
+            if step >= 2:
+                cross(a, order[step - 2])
                 if step < groups:
-                    between(step)
-
+                    between(step - 2)
+
+    load_projection()
     attend(0)
+    for a in range(1, HALVES):
+        load_cache(a)
     pl.semaphore_wait(barrier, len(greeted))
     project_out(0)
+    load_inward()
     attend(1)
+    load_down()
     share_hidden(0)
     project_out(1)
     norm_and_gather(0)
@@ -395,13 +404,14 @@
     pass_to_partner(0)
     take_from_partner(0)
     expert_rows(0)
-    down_out(0, lambda step: pass_to_partner(1) if step == groups else None)
+    down_out(0, lambda step: pass_to_partner(1) if step == groups - 1 else None)
     take_from_partner(1)
     expert_rows(1)
-    down_out(1, lambda step: finish(0, order[step - 1]))
-    for k in order:
+    down_out(1, lambda step: finish(0, order[step]))
+    for k in order[:-1]:
         finish(1, k)
     write(0)
+    finish(1, 0)
     write(1)
     for copy in sent:
         copy.wait_send()

time: 53 us -> 48.4 us (0.913)
  Pallas kernels: 51.3 us -> 46.7 us
    pallas_call x1, Pallas kernels: 51.3 us -> 46.7 us  [body(): pl.pallas_call(functools.partial(layer_kernel, pools, groups, experts), o...]
where the time goes in v5:
time: 48.4 us; the launch traced here: 48.2 us
  Pallas kernels  46.7 us (96%)
  other arithmetic  1.54 us (3%)
    pallas_call x1, Pallas kernels, body(): pl.pallas_call(functools.partial(layer_kernel, pools, groups, experts), o...  46.7 us
    convert_element_type x1, other arithmetic, body(): return summed.astype(BF16)  1.54 us

profile of v5, /device:TPU:0, one launch (start us, length us, event | category | flops | bytes accessed | tf_op | source)
XLA Modules:
  0.0 48.2 jit_solution(18185822627070946429)
XLA Ops:
  0.0 46.7 %shard_map.136 = f32[32,1024]{1,0:T(8,128)} custom-call(s32[32]{0:T(128)} %lengths_ref.1, bf16[32,1024]{1,0:T(8,128)(2,1)} %query_ref.1, bf16[32,128]{1,0:T(8,128)(2,1)} %new_key_ref.1, bf16[32,128]{1,0:T(8,128)(2,1)} %new_value_ref.1, bf16[32,4096]{1,0:T(8,128)(2,1)} %x_ref.1, s32[8,32]{1,0:T(8,128)} %bitcast.4, f32[8,32]{1,0:T(8,128)} %bitcast.5, ...), custom_call_target="tpu_custom_call" | custom-call | tf_op jit(solution)/shard_map/pallas_call | solution.py:453
  46.7 1.5 %convert_element_type.3 = bf16[32,1024]{1,0:T(8,128)(2,1)} convert(f32[32,1024]{1,0:T(8,128)} %shard_map.136) | non-fusion elementwise | flops 32768 | bytes 196608 | tf_op jit(solution)/shard_map/convert_element_type | solution.py:510

commit v6 on v5

--- a/solution.py
+++ b/solution.py
@@ -287,6 +287,12 @@
 
     block = min(16, pools)
 
+    def over_blocks(work):
+        if pools == block:
+            work(0, 0)
+        else:
+            lax.fori_loop(0, pools // block, work, 0)
+
     def expert_rows(a):
         if a == 0:
             for k in range(groups):
@@ -316,7 +322,7 @@
                 )
             return carry
 
-        lax.fori_loop(0, pools // block, some_rows, 0)
+        over_blocks(some_rows)
 
     def project_down(a, k):
         if a == 0:
@@ -333,7 +339,7 @@
             produced[a, k, place] = value.astype(BF16).reshape(block, half, share)
             return carry
 
-        lax.fori_loop(0, pools // block, some_rows, 0)
+        over_blocks(some_rows)
         swaps[a, k] = send(
             produced.at[a, k, pl.ds(chips, chips)],
             pair_recv.at[a, k],

time: 48.4 us -> 48.4 us (level)
  no operation moved by 1% of the time
where the time goes in v6:
time: 48.4 us; the launch traced here: 48.2 us
  Pallas kernels  46.7 us (96%)
  other arithmetic  1.54 us (3%)
    pallas_call x1, Pallas kernels, body(): pl.pallas_call(functools.partial(layer_kernel, pools, groups, experts), o...  46.7 us
    convert_element_type x1, other arithmetic, body(): return summed.astype(BF16)  1.54 us

profile of v6, /device:TPU:0, one launch (start us, length us, event | category | flops | bytes accessed | tf_op | source)
XLA Modules:
  0.0 48.2 jit_solution(18185822627070946429)
XLA Ops:
  0.0 46.7 %shard_map.136 = f32[32,1024]{1,0:T(8,128)} custom-call(s32[32]{0:T(128)} %lengths_ref.1, bf16[32,1024]{1,0:T(8,128)(2,1)} %query_ref.1, bf16[32,128]{1,0:T(8,128)(2,1)} %new_key_ref.1, bf16[32,128]{1,0:T(8,128)(2,1)} %new_value_ref.1, bf16[32,4096]{1,0:T(8,128)(2,1)} %x_ref.1, s32[8,32]{1,0:T(8,128)} %bitcast.4, f32[8,32]{1,0:T(8,128)} %bitcast.5, ...), custom_call_target="tpu_custom_call" | custom-call | tf_op jit(solution)/shard_map/pallas_call | solution.py:459
  46.7 1.5 %convert_element_type.3 = bf16[32,1024]{1,0:T(8,128)(2,1)} convert(f32[32,1024]{1,0:T(8,128)} %shard_map.136) | non-fusion elementwise | flops 32768 | bytes 196608 | tf_op jit(solution)/shard_map/convert_element_type | solution.py:516
